TPU v7x, 32 devices: a whole 2x2x4 slice. The times are simulated.
32 devices in a mesh: group: 2 (over y), expert: 4 (over z), dp: 4 (over x, core).
Axes of the slice: x: 2, y: 2, z: 4, core: 2. Of those that a mesh axis runs over, the one named last changes fastest.
Arguments:
- output_gradient: bfloat16 [1024, 4096], P(('group', 'expert'), 'dp'), parts along dimension 0, may hold values from -6 to 6
- routes: int32 [1024, 8], P(('group', 'expert')), parts along dimension 0, may hold values from 0 to 15, all different within a row; in each aligned block of 128 rows (0 to 127, 128 to 255, ...) at most 96 rows name the same one
- routing_weight_values: float32 [1024, 8], P(('group', 'expert')), parts along dimension 0, may hold values from 0 to 1, as said below
- stored_hidden_input: bfloat16 [32, 384, 768], P(('group', 'expert'), None, 'dp'), parts along dimension 0, may hold values from -6 to 6
- weight: bfloat16 [16, 768, 4096], P('expert', None, 'dp'), may hold values from -0.125 to 0.125
- output_channel_scale: float32 [16, 4096], P('expert', 'dp'), may hold values from 0.5 to 2
- adapter_down_matrix: bfloat16 [16, 768, 64], P('expert', 'dp'), may hold values from -0.21875 to 0.21875
- adapter_up_matrix: bfloat16 [16, 64, 4096], P('expert', None, 'dp'), may hold values from -0.09375 to 0.09375
Outputs:
- intermediate_derivative: bfloat16 [32, 384, 768], P(('group', 'expert'), None, 'dp'), parts along dimension 0
- reducer_factor_derivative: float32 [32, 768, 64], P(('group', 'expert'), 'dp'), parts along dimension 0
- expander_factor_derivative: float32 [32, 64, 4096], P(('group', 'expert'), None, 'dp'), parts along dimension 0
- router_score_derivative: float32 [1024, 8], P(('group', 'expert')), parts along dimension 0
There are 2 independent parts, one for each index of `group`. A program takes and returns all parts, laid end to end along the dimension named above; an argument that names none is the same for every part. Nothing has to cross between parts.
Inputs may be any that keep to these rules, and one draw needn't show every extreme that they name: `routes`: each token names 8 different experts. Among the tokens of one index of expert (aligned blocks of 128 tokens) no expert is named by more than 96 tokens, a bound that some block reaches. `routing_weight_values`: each row is positive and sums to one.
All inputs are finite; a program needn't handle non-finite values.
Results may differ from a plain program's by a relative error of at most 0.013.
Values may be sent and summed in bfloat16 or wider, within the bound.
A program may use at most 64 MiB of HBM per device.

v0:
```python
import jax
import jax.numpy as jnp
from jax import lax
from jax.sharding import PartitionSpec as P

correction_multiplier = 2.0


def local(
    output_gradient,
    routes,
    routing_weight_values,
    stored_hidden_input,
    weight,
    output_channel_scale,
    adapter_down_matrix,
    adapter_up_matrix,
):
    n_expert = lax.axis_size("expert")
    exp_dev = weight.shape[0]
    experts_all = exp_dev * n_expert
    slots = stored_hidden_input.shape[1]
    capacity = slots // n_expert
    tok_rows = routes.shape[0]
    top_count = routes.shape[1]
    width_part = output_gradient.shape[1]
    flat_routes = routes.reshape(-1)
    onehot = (flat_routes[:, None] == jnp.arange(experts_all, dtype=jnp.int32)[None, :]).astype(
        jnp.int32
    )
    ranks = jnp.sum(onehot * (jnp.cumsum(onehot, axis=0) - 1), axis=1)
    target = flat_routes * capacity + ranks
    pairs = tok_rows * top_count
    slot_source = (
        jnp.full((experts_all * capacity,), pairs, jnp.int32)
        .at[target]
        .set(jnp.arange(pairs, dtype=jnp.int32))
    )
    token_for_slot = slot_source // top_count
    padded_rows = jnp.concatenate(
        [output_gradient, jnp.zeros((1, width_part), output_gradient.dtype)], axis=0
    )
    send_rows = padded_rows[token_for_slot].reshape(experts_all, capacity, width_part)
    gate_bf = routing_weight_values.astype(jnp.bfloat16)
    padded_gates = jnp.concatenate([gate_bf.reshape(-1), jnp.zeros((1,), jnp.bfloat16)])
    send_gates = padded_gates[slot_source].reshape(experts_all, capacity)
    local_hproj = jnp.einsum(
        "mid,mda->mia", stored_hidden_input, adapter_down_matrix, preferred_element_type=jnp.float32
    )
    incoming_derivative_lines, slot_gate_weights = (
        lax.all_to_all(send_rows, "expert", split_axis=0, concat_axis=1, tiled=True),
        lax.all_to_all(send_gates, "expert", split_axis=0, concat_axis=1, tiled=True),
    )
    scaled = (
        incoming_derivative_lines.astype(jnp.float32) * output_channel_scale[:, None, :]
    ).astype(jnp.bfloat16)
    frozen_t = lax.psum_scatter(
        jnp.einsum("esd,efd->fes", scaled, weight, preferred_element_type=jnp.float32).astype(
            jnp.bfloat16
        ),
        "dp",
        scatter_dimension=0,
        tiled=True,
    ).astype(jnp.float32)
    frozen_contribution = jnp.transpose(frozen_t, (1, 2, 0))
    local_row_projection = jnp.einsum(
        "awy,agy->awg",
        incoming_derivative_lines,
        adapter_up_matrix,
        preferred_element_type=jnp.float32,
    )
    row_proj_f, hidden_proj = (
        lax.psum(local_row_projection.astype(jnp.bfloat16), "dp").astype(jnp.float32),
        lax.psum(local_hproj.astype(jnp.bfloat16), "dp").astype(jnp.float32),
    )
    row_projection = row_proj_f.astype(jnp.bfloat16)
    hidden_unit_gradient = frozen_contribution + correction_multiplier * jnp.einsum(
        "jkh,jzh->jkz", row_projection, adapter_down_matrix, preferred_element_type=jnp.float32
    )
    gate_col = slot_gate_weights.astype(jnp.float32)[:, :, None]
    intermediate_derivative = (gate_col * hidden_unit_gradient).astype(jnp.bfloat16)
    gate_part = jnp.sum(stored_hidden_input.astype(jnp.float32) * hidden_unit_gradient, axis=2)
    mapped_weighted_product = (gate_col * row_projection.astype(jnp.float32)).astype(jnp.bfloat16)
    reducer_factor_derivative = correction_multiplier * jnp.einsum(
        "esf,esr->efr",
        stored_hidden_input,
        mapped_weighted_product,
        preferred_element_type=jnp.float32,
    )
    intermediate_weighted_product = (gate_col * hidden_proj).astype(jnp.bfloat16)
    expander_factor_derivative = correction_multiplier * jnp.einsum(
        "esr,esd->erd",
        intermediate_weighted_product,
        incoming_derivative_lines,
        preferred_element_type=jnp.float32,
    )
    summed = lax.psum(gate_part, "dp")
    returned = lax.all_to_all(summed, "expert", split_axis=1, concat_axis=0, tiled=True)
    pair_dgate = returned.reshape(-1)[target].reshape(tok_rows, top_count)
    mean_term = jnp.sum(routing_weight_values * pair_dgate, axis=1, keepdims=True)
    router_score_derivative = routing_weight_values * (pair_dgate - mean_term)
    return (
        intermediate_derivative,
        reducer_factor_derivative,
        expander_factor_derivative,
        router_score_derivative,
    )


def solution(mesh):
    return jax.shard_map(
        local,
        mesh=mesh,
        in_specs=(
            P(("group", "expert"), "dp"),
            P(("group", "expert"), None),
            P(("group", "expert"), None),
            P(("group", "expert"), None, "dp"),
            P("expert", None, "dp"),
            P("expert", "dp"),
            P("expert", "dp", None),
            P("expert", None, "dp"),
        ),
        out_specs=(
            P(("group", "expert"), None, "dp"),
            P(("group", "expert"), "dp", None),
            P(("group", "expert"), None, "dp"),
            P(("group", "expert"), None),
        ),
        check_vma=False,
    )
```

profile of v0, /device:TPU:0, one launch (start us, length us, event | category | flops | bytes accessed | tf_op | source)
XLA Modules:
  0.0 216.2 jit_solution(17003968262829490000)
XLA Ops:
  7.2 0.7 broadcast_multiply_fusion
  7.9 0.8 copy.47
  9.1 4.5 %reduce-window.6 = s32[16,8,128]{2,1,0:T(8,128)S(1)} reduce-window(s32[16,8,128]{2,1,0:T(8,128)S(1)} %fusion.8, s32[]{:T(128)} %constant.12.clone.1), window={size=1x1x128 pad=0_0x0_0x127_0}, to_apply=%region_0.0 | reduce-window | flops 2080768 | bytes 131076 | tf_op jit(solution)/shard_map/reduce-window
  13.7 0.1 copy.49
  14.1 4.3 %scatter_custom_fusion = s32[1536]{0:T(1024)S(1)} fusion(s32[1024]{0:T(1024)S(1)} %bitcast.48, s32[1024]{0:T(1024)S(1)} %iota.11, s32[]{:T(128)} %constant.15.clone.1), kind=kCustom, calls=%fused_computation.44 | custom fusion | bytes 6148 | tf_op jit(solution)/shard_map/scatter | solution.py:37
  18.5 1.0 concatenate.7
  19.4 5.8 %gather_fusion.1 = bf16[1536,1024]{1,0:T(8,128)(2,1)} fusion(bf16[129,1024]{1,0:T(8,128)(2,1)S(1)} %concatenate.7, s32[2048]{0:T(1024)S(1)} %get-tuple-element.27), kind=kCustom, calls=%fused_computation.1 | custom fusion | bytes 6297600 | tf_op jit(solution)/shard_map/gather | solution.py:43
  25.3 6.4 %all-to-all-start.1 = ((bf16[16,96,1024]{2,1,0:T(8,128)(2,1)}), bf16[16,96,1024]{2,1,0:T(8,128)(2,1)}, u32[]{:S(2)}, u32[]{:S(2)}) async-start(bf16[16,96,1024]{2,1,0:T(8,128)(2,1)} %bitcast.43), calls=%async_computation.1 | async-start | bytes 6291456 | tf_op jit(solution)/shard_map/all_to_all | solution.py:51
  31.7 0.9 convolution_convert_fusion
  32.7 69.8 %all-to-all-done.1 = bf16[16,96,1024]{2,1,0:T(8,128)(2,1)} async-done(((bf16[16,96,1024]{2,1,0:T(8,128)(2,1)}), bf16[16,96,1024]{2,1,0:T(8,128)(2,1)}, u32[]{:S(2)}, u32[]{:S(2)}) %all-to-all-start.1) | async-done | bytes 3145760 | tf_op jit(solution)/shard_map/all_to_all | solution.py:51
  102.5 2.2 %copy.52 = bf16[4,4,96,1024]{3,2,1,0:T(8,128)(2,1)S(1)} copy(bf16[4,4,96,1024]{3,2,0,1:T(8,128)(2,1)} %bitcast.7) | data formatting | bytes 6291456 | tf_op jit(solution)/shard_map/all_to_all | solution.py:51
  104.7 1.8 convolution_convert_fusion.1
  106.5 7.2 %convert_bitcast_fusion = bf16[768,4,384]{0,2,1:T(8,128)(2,1)S(1)} fusion(bf16[4,768,1024]{2,1,0:T(8,128)(2,1)} %param.12, bf16[4,384,1024]{2,1,0:T(8,128)(2,1)S(1)} %bitcast.41, f32[4,1024]{1,0:T(4,128)S(1)} %copy-done.7), kind=kOutput, calls=%fused_computation.7 | convolution fusion | flops 2421817344 | bytes 11812864 | tf_op jit(solution)/shard_map/esd,efd->fes/dot_general | solution.py:58
  113.8 3.4 %copy.53 = bf16[768,4,384]{2,1,0:T(4,128)(2,1)} copy(bf16[768,4,384]{0,2,1:T(8,128)(2,1)S(1)} %convert_bitcast_fusion) | data formatting | bytes 4718592 | tf_op jit(solution)/shard_map/convert_element_type | solution.py:58
  117.2 0.1 copy.45
  117.4 0.1 reshape.86
  117.5 9.5 %gather_fusion = bf16[1536]{0:T(1024)(128)(2,1)S(1)} fusion(bf16[1025]{0:T(1024)(128)(2,1)S(1)} %pad_maximum_fusion, s32[2048]{0:T(1024)S(1)} %get-tuple-element.28), kind=kCustom, calls=%fused_computation | custom fusion | bytes 12288 | tf_op jit(solution)/shard_map/gather | solution.py:46
  127.0 0.7 all_to_all.35
  127.6 3.2 %all-to-all-start = ((bf16[4,4,96]{2,1,0:T(4,128)(2,1)}), bf16[4,4,96]{2,1,0:T(4,128)(2,1)S(1)}, u32[]{:S(2)}, u32[]{:S(2)}) async-start(bf16[4,4,96]{2,1,0:T(4,128)(2,1)} %all_to_all.35), calls=%async_computation | async-start | bytes 8192 | tf_op jit(solution)/shard_map/all_to_all | solution.py:52
  131.0 0.6 dynamic-slice
  132.3 4.2 %all-to-all-done = bf16[4,4,96]{2,1,0:T(4,128)(2,1)S(1)} async-done(((bf16[4,4,96]{2,1,0:T(4,128)(2,1)}), bf16[4,4,96]{2,1,0:T(4,128)(2,1)S(1)}, u32[]{:S(2)}, u32[]{:S(2)}) %all-to-all-start) | async-done | bytes 3104 | tf_op jit(solution)/shard_map/all_to_all | solution.py:52
  136.5 42.4 %all-reduce.5.cloned.1.call-done = (bf16[4,384,64]{1,2,0:T(8,128)(2,1)}, bf16[768,4,384]{2,1,0:T(4,128)(2,1)}, bf16[4,384,64]{1,2,0:T(8,128)(2,1)}) async-done(((bf16[4,384,64]{1,2,0:T(8,128)(2,1)}, bf16[768,4,384]{2,1,0:T(4,128)(2,1)}, bf16[4,384,64]{1,2,0:T(8,128)(2,1)}), (bf16[4,384,64]{1,2,0:T(8,128)(2,1)}, bf16[768,4,384]{2,1,0:T(4,128)(2,1)}, ...) | async-done | bytes 2752528 | tf_op jit(solution)/shard_map/psum | solution.py:73
  178.9 1.3 constant_dynamic-slice_fusion
  180.2 3.7 %convolution_multiply_fusion.1 = f32[4,64,1024]{2,1,0:T(8,128)} fusion(bf16[4,384,1024]{2,1,0:T(8,128)(2,1)} %bitcast.42, bf16[4,384,64]{1,2,0:T(8,128)(2,1)} %get-tuple-element.22, f32[4,384]{1,0:T(4,128)S(1)} %reshape.91), kind=kOutput, calls=%fused_computation.10 | convolution fusion | flops 201883648 | bytes 4397056 | tf_op jit(solution)/shard_map/esr,esd->erd/dot_general | solution.py:91
  183.9 1.3 multiply_reduce_fusion
  185.3 5.9 %psum.23 = f32[4,4,96]{2,1,0:T(4,128)S(1)} all-reduce(f32[4,4,96]{2,1,0:T(4,128)S(1)} %all_to_all.41), channel_id=1, replica_groups=mesh['group'=2,'expert'=4,'dp'=4] {'dp'}, use_global_device_ids=true, to_apply=%region_8.9 | all-reduce | flops 1536 | bytes 12288 | tf_op jit(solution)/shard_map/psum | solution.py:97
  191.1 0.6 copy.55
  191.7 4.8 %all-to-all-start.2 = ((f32[4,4,96]{2,0,1:T(4,128)}), f32[4,4,96]{2,0,1:T(4,128)S(1)}, u32[]{:S(2)}, u32[]{:S(2)}) async-start(f32[4,4,96]{2,0,1:T(4,128)} %copy.55), calls=%async_computation.2 | async-start | bytes 16384 | tf_op jit(solution)/shard_map/all_to_all | solution.py:98
  196.6 1.1 fusion.3
  197.6 4.5 %all-to-all-done.2 = f32[4,4,96]{2,0,1:T(4,128)S(1)} async-done(((f32[4,4,96]{2,0,1:T(4,128)}), f32[4,4,96]{2,0,1:T(4,128)S(1)}, u32[]{:S(2)}, u32[]{:S(2)}) %all-to-all-start.2) | async-done | bytes 6176 | tf_op jit(solution)/shard_map/all_to_all | solution.py:98
  202.2 6.1 %gather_fusion.2 = f32[1024]{0:T(1024)S(1)} fusion(f32[1536]{0:T(1024)S(1)} %reshape.89, s32[1024]{0:T(1024)S(1)} %broadcast_clamp_fusion), kind=kCustom, calls=%fused_computation.2 | custom fusion | bytes 12288 | tf_op jit(solution)/shard_map/gather | solution.py:99
  208.7 0.7 copy.58
  (47 shorter events, 1.4 us)
Async XLA Ops:
  7.2 97.6 %copy-start = (bf16[4,64,1024]{2,1,0:T(8,128)(2,1)S(1)}, bf16[4,64,1024]{2,1,0:T(8,128)(2,1)}, u32[]{:S(2)}) copy-start(bf16[4,64,1024]{2,1,0:T(8,128)(2,1)} %param.15) | copy-start | bytes 1572868
  25.3 6.5 %copy-start.2 = (bf16[4,384,192]{1,2,0:T(8,128)(2,1)S(1)}, bf16[4,384,192]{1,2,0:T(8,128)(2,1)}, u32[]{:S(2)}) copy-start(bf16[4,384,192]{1,2,0:T(8,128)(2,1)} %param.11) | copy-start | bytes 1769476
  25.3 6.5 %copy-start.4 = (bf16[4,192,64]{1,2,0:T(8,128)(2,1)S(1)}, bf16[4,192,64]{1,2,0:T(8,128)(2,1)}, u32[]{:S(2)}) copy-start(bf16[4,192,64]{1,2,0:T(8,128)(2,1)} %param.14) | copy-start | bytes 294916
  25.3 77.2 %all-to-all-start.1 = ((bf16[16,96,1024]{2,1,0:T(8,128)(2,1)}), bf16[16,96,1024]{2,1,0:T(8,128)(2,1)}, u32[]{:S(2)}, u32[]{:S(2)}) async-start(bf16[16,96,1024]{2,1,0:T(8,128)(2,1)} %bitcast.43), calls=%async_computation.1 | async-start | bytes 6291456 | tf_op jit(solution)/shard_map/all_to_all | solution.py:51
  31.7 147.2 %all-reduce.5.cloned.1.call-start = ((), (), s32[]{:S(2)}) async-start(), calls=%async_computation.3 | async-start | bytes 5505024 | tf_op jit(solution)/shard_map/psum | solution.py:73
  104.7 1.8 copy-start.1
  104.7 1.8 copy-start.7
  113.7 3.5 %copy-start.6 = (f32[128,8]{0,1:T(8,128)S(1)}, f32[128,8]{0,1:T(8,128)}, u32[]{:S(2)}) copy-start(f32[128,8]{0,1:T(8,128)} %param.10) | copy-start | bytes 12292
  117.2 13.8 %copy-start.8 = (u32[32]{0:T(128)S(1)}, u32[32]{0:T(128)}, u32[]{:S(2)}) copy-start(u32[32]{0:T(128)} %constant.50) | copy-start | bytes 388
  126.9 56.9 %copy-start.5 = (bf16[4,192,64]{1,2,0:T(8,128)(2,1)S(1)}, bf16[4,192,64]{1,2,0:T(8,128)(2,1)}, u32[]{:S(2)}) copy-start(bf16[4,192,64]{1,2,0:T(8,128)(2,1)} %param.14) | copy-start | bytes 294916
  127.6 8.8 %all-to-all-start = ((bf16[4,4,96]{2,1,0:T(4,128)(2,1)}), bf16[4,4,96]{2,1,0:T(4,128)(2,1)S(1)}, u32[]{:S(2)}, u32[]{:S(2)}) async-start(bf16[4,4,96]{2,1,0:T(4,128)(2,1)} %all_to_all.35), calls=%async_computation | async-start | bytes 8192 | tf_op jit(solution)/shard_map/all_to_all | solution.py:52
  178.9 5.0 %copy-start.3 = (bf16[4,384,64]{1,2,0:T(8,128)(2,1)S(1)}, bf16[4,384,64]{1,2,0:T(8,128)(2,1)}, u32[]{:S(2)}) copy-start(bf16[4,384,64]{1,2,0:T(8,128)(2,1)} %get-tuple-element.20) | copy-start | bytes 589828
  191.7 10.4 %all-to-all-start.2 = ((f32[4,4,96]{2,0,1:T(4,128)}), f32[4,4,96]{2,0,1:T(4,128)S(1)}, u32[]{:S(2)}, u32[]{:S(2)}) async-start(f32[4,4,96]{2,0,1:T(4,128)} %copy.55), calls=%async_computation.2 | async-start | bytes 16384 | tf_op jit(solution)/shard_map/all_to_all | solution.py:98
Sparse Core Ops, SparseCore 0:
  117.3 61.5 all-reduce.4
where the time goes:
time: 217 us; the launch traced here: 216 us
  waiting for transfers between devices  121 us (56%)
  local copies, waits for them, and re-layouts  38.3 us (18%)
  matrix products  16 us (7%)
  between operations  14.9 us (7%)
  starting transfers between devices  14.5 us (7%)
  blocking collectives  5.86 us (3%)
  other arithmetic  5.66 us (3%)
    all_to_all x1, waiting for transfers between devices, local(): lax.all_to_all(send_rows, 'expert', split_axis=0, concat_axis=1, tiled=True)  69.8 us
    psum x1, waiting for transfers between devices, local(): lax.psum(local_row_projection.astype(jnp.bfloat16), 'dp')  42.4 us
    gather x1, local copies, waits for them, and re-layouts, local(): send_gates = padded_gates[slot_source].reshape(experts_all, capacity)  9.46 us
    dot_general x1, matrix products, local(): jnp.einsum('esd,efd->fes', scaled, weight, preferred_element_type=jnp.flo...  7.24 us
    all_to_all x1, starting transfers between devices, local(): lax.all_to_all(send_rows, 'expert', split_axis=0, concat_axis=1, tiled=True)  6.45 us
    gather x1, local copies, waits for them, and re-layouts, local(): pair_dgate = returned.reshape(-1)[target].reshape(tok_rows, top_count)  6.15 us
    psum x1, blocking collectives, local(): summed = lax.psum(gate_part, 'dp')  5.86 us
    gather x1, local copies, waits for them, and re-layouts, local(): padded_rows[token_for_slot].reshape(experts_all, capacity, width_part)  5.83 us
  transfers between devices with their start and end apart: 4, of which 4 were waited for; matrix products, arithmetic and copies ran while one was open for 6% of the time, Pallas kernels for 0%

commit v1 on v0

v1 whole, which is shorter than its diff:
```python
import jax
import jax.numpy as jnp
from jax import lax
from jax.sharding import PartitionSpec as P

correction_multiplier = 2.0


def local(
    output_gradient,
    routes,
    routing_weight_values,
    stored_hidden_input,
    weight,
    output_channel_scale,
    adapter_down_matrix,
    adapter_up_matrix,
):
    n_expert = lax.axis_size("expert")
    exp_dev = weight.shape[0]
    experts_all = exp_dev * n_expert
    slots = stored_hidden_input.shape[1]
    capacity = slots // n_expert
    tok_rows, top_count = routes.shape
    width_part = output_gradient.shape[1]
    bf16, f32 = jnp.bfloat16, jnp.float32

    packed = jnp.concatenate(
        [output_gradient, routes.astype(bf16), routing_weight_values.astype(bf16)], axis=1
    )
    everyone = lax.all_gather(packed, "expert", axis=0, tiled=True)
    rows_all = everyone[:, :width_part]
    routes_all = everyone[:, width_part : width_part + top_count].astype(f32).astype(jnp.int32)
    gates_all = everyone[:, width_part + top_count :].astype(f32)
    hidden_local = jnp.einsum(
        "mid,mda->mia", stored_hidden_input, adapter_down_matrix, preferred_element_type=f32
    )
    mine = lax.axis_index("expert") * exp_dev + jnp.arange(exp_dev, dtype=jnp.int32)
    hit = routes_all[None, :, :] == mine[:, None, None]
    named = jnp.any(hit, axis=2)
    token_gate = jnp.sum(jnp.where(hit, gates_all[None], 0.0), axis=2)
    before = (
        jnp.arange(tok_rows)[:, None] > jnp.arange(tok_rows)[None, :]
    ).astype(bf16)
    ranks = jnp.einsum(
        "ent,ut->enu",
        named.astype(bf16).reshape(exp_dev, n_expert, tok_rows),
        before,
        preferred_element_type=f32,
    ).astype(jnp.int32)
    slot = ranks + capacity * jnp.arange(n_expert, dtype=jnp.int32)[None, :, None]
    slot = jnp.where(named, slot.reshape(exp_dev, -1), -1)
    place = slot[:, None, :] == jnp.arange(slots, dtype=jnp.int32)[None, :, None]
    lines = jnp.einsum(
        "est,td->esd", place.astype(bf16), rows_all, preferred_element_type=f32
    ).astype(bf16)
    gate_col = jnp.sum(jnp.where(place, token_gate[:, None, :], 0.0), axis=2)[:, :, None]

    scaled = (lines.astype(f32) * output_channel_scale[:, None, :]).astype(bf16)
    row_local = jnp.einsum("awy,agy->awg", lines, adapter_up_matrix, preferred_element_type=f32)
    both = lax.psum(
        jnp.concatenate([row_local, hidden_local], axis=2).astype(bf16), "dp"
    )
    rank_count = adapter_up_matrix.shape[1]
    row_projection = both[:, :, :rank_count]
    hidden_proj = both[:, :, rank_count:].astype(f32)
    frozen_t = lax.psum_scatter(
        jnp.einsum("esd,efd->fes", scaled, weight, preferred_element_type=f32).astype(bf16),
        "dp",
        scatter_dimension=0,
        tiled=True,
    ).astype(f32)
    frozen_contribution = jnp.transpose(frozen_t, (1, 2, 0))
    hidden_unit_gradient = frozen_contribution + correction_multiplier * jnp.einsum(
        "jkh,jzh->jkz", row_projection, adapter_down_matrix, preferred_element_type=f32
    )
    intermediate_derivative = (gate_col * hidden_unit_gradient).astype(bf16)
    gate_part = jnp.sum(stored_hidden_input.astype(f32) * hidden_unit_gradient, axis=2)
    gated_proj = (gate_col * row_projection.astype(f32)).astype(bf16)
    reducer_factor_derivative = correction_multiplier * jnp.einsum(
        "esf,esr->efr", stored_hidden_input, gated_proj, preferred_element_type=f32
    )
    gated_hidden = (gate_col * hidden_proj).astype(bf16)
    expander_factor_derivative = correction_multiplier * jnp.einsum(
        "esr,esd->erd", gated_hidden, lines, preferred_element_type=f32
    )
    token_dgate = jnp.sum(jnp.where(place, gate_part[:, :, None], 0.0), axis=1)
    returned = lax.all_to_all(
        token_dgate.reshape(exp_dev, n_expert, tok_rows),
        "expert",
        split_axis=1,
        concat_axis=0,
        tiled=True,
    ).reshape(experts_all, tok_rows)
    summed = lax.psum(returned, "dp")
    named_by = routes.T[:, None, :] == jnp.arange(experts_all, dtype=jnp.int32)[None, :, None]
    pair_dgate = jnp.sum(jnp.where(named_by, summed[None], 0.0), axis=1).T
    mean_term = jnp.sum(routing_weight_values * pair_dgate, axis=1, keepdims=True)
    router_score_derivative = routing_weight_values * (pair_dgate - mean_term)
    return (
        intermediate_derivative,
        reducer_factor_derivative,
        expander_factor_derivative,
        router_score_derivative,
    )


def solution(mesh):
    return jax.shard_map(
        local,
        mesh=mesh,
        in_specs=(
            P(("group", "expert"), "dp"),
            P(("group", "expert"), None),
            P(("group", "expert"), None),
            P(("group", "expert"), None, "dp"),
            P("expert", None, "dp"),
            P("expert", "dp"),
            P("expert", "dp", None),
            P("expert", None, "dp"),
        ),
        out_specs=(
            P(("group", "expert"), None, "dp"),
            P(("group", "expert"), "dp", None),
            P(("group", "expert"), None, "dp"),
            P(("group", "expert"), None),
        ),
        check_vma=False,
    )
```

time: 217 us -> 153 us (0.71)
  local copies, waits for them, and re-layouts: 38.3 us -> 7.15 us
  waiting for transfers between devices: 121 us -> 95.7 us
  starting transfers between devices: 14.5 us -> 4.68 us
    all_to_all x3 -> x1, waiting for transfers between devices: 78.5 us -> 4.51 us  [local(): lax.all_to_all(token_dgate.reshape(exp_dev, n_expert, tok_rows), 'expert'...]
    unnamed x1 -> x3, waiting for transfers between devices: 0.02 us -> 59.4 us
    psum x1 -> x0, waiting for transfers between devices: 42.4 us -> none  [local(): lax.psum(local_row_projection.astype(jnp.bfloat16), 'dp')]
    all_gather x0 -> x1, waiting for transfers between devices: none -> 31.8 us  [local(): everyone = lax.all_gather(packed, 'expert', axis=0, tiled=True)]
    gather x3 -> x0, local copies, waits for them, and re-layouts: 21.4 us -> none  [the longest x1 9.46 us: local(): send_gates = padded_gates[slot_source].reshape(experts_all, capacity)]
    all_to_all x3 -> x1, starting transfers between devices: 14.5 us -> 4.6 us  [local(): lax.all_to_all(token_dgate.reshape(exp_dev, n_expert, tok_rows), 'expert'...]
    another operation x2 -> x0, other arithmetic: 4.55 us -> none
    scatter x1 -> x0, local copies, waits for them, and re-layouts: 4.32 us -> none  [local(): slot_source = jnp.full((experts_all * capacity,), pairs, jnp.int32).at[ta...]
  transfers between devices with their start and end apart: 4 -> 3, of which waited for: 4 -> 3; matrix products, arithmetic and copies ran while one was open for 6% -> 2% of each run, Pallas kernels for 0% -> 0%
where the time goes in v1:
time: 153 us; the launch traced here: 152 us
  waiting for transfers between devices  95.7 us (63%)
  matrix products  17 us (11%)
  between operations  14.9 us (10%)
  local copies, waits for them, and re-layouts  7.15 us (5%)
  other arithmetic  7.03 us (5%)
  blocking collectives  6.05 us (4%)
  starting transfers between devices  4.68 us (3%)
    unnamed x3, waiting for transfers between devices  59.4 us
    all_gather x1, waiting for transfers between devices, local(): everyone = lax.all_gather(packed, 'expert', axis=0, tiled=True)  31.8 us
    dot_general x1, matrix products, local(): jnp.einsum('esd,efd->fes', scaled, weight, preferred_element_type=f32)  7.23 us
    psum x1, blocking collectives, local(): summed = lax.psum(returned, 'dp')  6.05 us
    all_to_all x1, starting transfers between devices, local(): lax.all_to_all(token_dgate.reshape(exp_dev, n_expert, tok_rows), 'expert'...  4.6 us
    all_to_all x1, waiting for transfers between devices, local(): lax.all_to_all(token_dgate.reshape(exp_dev, n_expert, tok_rows), 'expert'...  4.51 us
    unnamed x23, local copies, waits for them, and re-layouts  3.72 us
    convert_element_type x1, local copies, waits for them, and re-layouts, local(): jnp.einsum('esd,efd->fes', scaled, weight, preferred_element_type=f32)  3.42 us
  transfers between devices with their start and end apart: 3, of which 3 were waited for; matrix products, arithmetic and copies ran while one was open for 2% of the time, Pallas kernels for 0%

profile of v1, /device:TPU:0, one launch (start us, length us, event | category | flops | bytes accessed | tf_op | source)
XLA Modules:
  0.0 152.4 jit_solution(10467026850509312290)
XLA Ops:
  7.2 0.0 all-gather.2.cloned.1.call-start
  7.2 0.7 convert_element_type.56
  8.0 0.7 convert_element_type.57
  8.7 1.1 copy.27
  9.8 0.7 pad_maximum_fusion.1
  10.5 0.0 all-gather.2.cloned.1.call-update
  10.5 0.0 all-reduce.4.cloned.1.call-start
  10.6 1.4 convolution_convert_fusion
  12.0 31.8 %all-gather.2.cloned.1.call-done = bf16[512,1040]{0,1:T(8,128)(2,1)} async-done(((bf16[128,1040]{0,1:T(8,128)(2,1)}), bf16[512,1040]{0,1:T(8,128)(2,1)}) %all-gather.2.cloned.1.call-update) | async-done | bytes 1064976 | tf_op jit(solution)/shard_map/all_gather | solution.py:31
  43.8 0.7 slice_convert_fusion
  44.5 0.1 compare_reduce_fusion
  44.6 0.1 fusion.8
  44.8 3.1 %fusion.3 = bf16[4,384,1024]{2,1,0:T(8,128)(2,1)S(1)} fusion(s32[4,512]{1,0:T(4,128)S(1)} %bitcast_select_fusion, bf16[512,1040]{0,1:T(8,128)(2,1)} %all-gather.2.cloned.1.call-done), kind=kOutput, calls=%fused_computation.8 | convolution fusion | flops 1612972032 | bytes 4202496 | tf_op jit(solution)/shard_map/est,td->esd/dot_general | solution.py:54
  47.9 1.1 convolution_convert_fusion.1
  49.0 0.6 copy-done.1
  49.6 7.2 %convert_bitcast_fusion = bf16[768,4,384]{0,2,1:T(8,128)(2,1)S(1)} fusion(bf16[4,768,1024]{2,1,0:T(8,128)(2,1)} %param.12, bf16[4,384,1024]{2,1,0:T(8,128)(2,1)S(1)} %fusion.3, f32[4,1024]{1,0:T(4,128)S(1)} %copy-done.8), kind=kOutput, calls=%fused_computation.7 | convolution fusion | flops 2421817344 | bytes 11812864 | tf_op jit(solution)/shard_map/esd,efd->fes/dot_general | solution.py:68
  56.8 3.4 %copy.29 = bf16[768,4,384]{2,1,0:T(4,128)(2,1)} copy(bf16[768,4,384]{0,2,1:T(8,128)(2,1)S(1)} %convert_bitcast_fusion) | data formatting | bytes 4718592 | tf_op jit(solution)/shard_map/convert_element_type | solution.py:68
  60.2 0.8 pad_maximum_fusion
  61.0 0.0 all-reduce.4.cloned.1.call-update
  61.1 0.6 dynamic-slice
  62.3 0.1 fusion.14
  62.4 59.3 %all-reduce.4.cloned.1.call-done = (bf16[768,4,384]{2,1,0:T(4,128)(2,1)}, bf16[4,384,128]{1,2,0:T(8,128)(2,1)}) async-done(((bf16[768,4,384]{2,1,0:T(4,128)(2,1)}, bf16[4,384,128]{1,2,0:T(8,128)(2,1)}), (bf16[768,4,384]{2,1,0:T(4,128)(2,1)}, bf16[4,384,128]{1,2,0:T(8,128)(2,1)})) %all-reduce.4.cloned.1.call-update) | async-done | bytes 2752528
  121.7 1.4 constant_dynamic-slice_fusion
  123.2 1.3 multiply_reduce_fusion
  124.5 1.6 %select_reduce_fusion = (f32[4,512]{1,0:T(4,128)}, f32[4,384]{1,0:T(4,128)S(1)}) fusion(f32[4,384]{1,0:T(4,128)S(1)} %get-tuple-element.14, s32[4,512]{1,0:T(4,128)S(1)} %bitcast_select_fusion, f32[4,512]{1,0:T(4,128)S(1)} %fusion.14), kind=kLoop, calls=%fused_computation.2 | loop fusion | flops 3928576 | bytes 36864 | tf_op jit(solution)/shard_map/reduce_sum | solution.py:87
  126.1 1.7 %convolution_multiply_fusion.1 = f32[4,64,1024]{2,1,0:T(8,128)} fusion(bf16[4,384,1024]{2,1,0:T(8,128)(2,1)S(1)} %copy-done.2, bf16[4,384,128]{1,2,0:T(8,128)(2,1)S(1)} %copy-done.4, f32[4,384]{1,0:T(4,128)S(1)} %get-tuple-element.9), kind=kOutput, calls=%fused_computation.12 | convolution fusion | flops 201883648 | bytes 4397056 | tf_op jit(solution)/shard_map/esr,esd->erd/dot_general | solution.py:84
  127.8 0.9 multiply_convert_fusion.4
  128.7 4.6 %all-to-all-start = ((f32[4,4,128]{2,0,1:T(4,128)}), f32[4,4,128]{2,0,1:T(4,128)S(1)}, u32[]{:S(2)}, u32[]{:S(2)}) async-start(f32[4,4,128]{2,0,1:T(4,128)} %bitcast.6), calls=%async_computation | async-start | bytes 16384 | tf_op jit(solution)/shard_map/all_to_all | solution.py:88
  133.3 1.1 fusion.6
  134.3 4.5 %all-to-all-done = f32[4,4,128]{2,0,1:T(4,128)S(1)} async-done(((f32[4,4,128]{2,0,1:T(4,128)}), f32[4,4,128]{2,0,1:T(4,128)S(1)}, u32[]{:S(2)}, u32[]{:S(2)}) %all-to-all-start) | async-done | bytes 8224 | tf_op jit(solution)/shard_map/all_to_all | solution.py:88
  138.9 6.0 %psum.15 = f32[16,128]{1,0:T(8,128)S(1)} all-reduce(f32[16,128]{1,0:T(8,128)S(1)} %bitcast.40), channel_id=1, replica_groups=mesh['group'=2,'expert'=4,'dp'=4] {'dp'}, use_global_device_ids=true, to_apply=%region_7.8 | all-reduce | flops 2048 | bytes 16384 | tf_op jit(solution)/shard_map/psum | solution.py:95
  145.0 0.6 fusion.18
  (25 shorter events, 0.2 us)
Async XLA Ops:
  7.2 40.7 %copy-start = (bf16[4,64,1024]{2,1,0:T(8,128)(2,1)S(1)}, bf16[4,64,1024]{2,1,0:T(8,128)(2,1)}, u32[]{:S(2)}) copy-start(bf16[4,64,1024]{2,1,0:T(8,128)(2,1)} %param.15) | copy-start | bytes 1572868
  7.2 36.6 %all-gather.2.cloned.1.call-start = ((), (), s32[]{:S(2)}) async-start(), calls=%async_computation.1 | async-start | bytes 1331200 | tf_op jit(solution)/shard_map/all_gather | solution.py:31
  10.5 111.2 %all-reduce.4.cloned.1.call-start = ((), (), s32[]{:S(2)}) async-start(), calls=%async_computation.2 | async-start | bytes 5505024
  47.9 1.7 %copy-start.1 = (bf16[4,384,1024]{2,1,0:T(8,128)(2,1)}, bf16[4,384,1024]{2,1,0:T(8,128)(2,1)S(1)}, u32[]{:S(2)}) copy-start(bf16[4,384,1024]{2,1,0:T(8,128)(2,1)S(1)} %fusion.3) | copy-start | bytes 9437188
  47.9 1.7 %copy-start.8 = (f32[4,1024]{1,0:T(4,128)S(1)}, f32[4,1024]{1,0:T(4,128)}, u32[]{:S(2)}) copy-start(f32[4,1024]{1,0:T(4,128)} %param.13) | copy-start | bytes 49156
  56.8 4.3 %copy-start.9 = (u32[32]{0:T(128)S(1)}, u32[32]{0:T(128)}, u32[]{:S(2)}) copy-start(u32[32]{0:T(128)} %constant.22) | copy-start | bytes 388
  60.2 62.9 %copy-start.3 = (bf16[4,384,192]{1,2,0:T(8,128)(2,1)S(1)}, bf16[4,384,192]{1,2,0:T(8,128)(2,1)}, u32[]{:S(2)}) copy-start(bf16[4,384,192]{1,2,0:T(8,128)(2,1)} %param.11) | copy-start | bytes 1769476
  60.2 62.9 %copy-start.5 = (bf16[4,192,64]{1,2,0:T(8,128)(2,1)S(1)}, bf16[4,192,64]{1,2,0:T(8,128)(2,1)}, u32[]{:S(2)}) copy-start(bf16[4,192,64]{1,2,0:T(8,128)(2,1)} %param.14) | copy-start | bytes 294916
  121.7 4.4 %copy-start.2 = (bf16[4,384,1024]{2,1,0:T(8,128)(2,1)S(1)}, bf16[4,384,1024]{2,1,0:T(8,128)(2,1)}, u32[]{:S(2)}) copy-start(bf16[4,384,1024]{2,1,0:T(8,128)(2,1)} %copy-done.1) | copy-start | bytes 9437188
  121.7 4.4 %copy-start.4 = (bf16[4,384,128]{1,2,0:T(8,128)(2,1)S(1)}, bf16[4,384,128]{1,2,0:T(8,128)(2,1)}, u32[]{:S(2)}) copy-start(bf16[4,384,128]{1,2,0:T(8,128)(2,1)} %get-tuple-element.11) | copy-start | bytes 1179652
  126.1 18.8 %copy-start.7 = (s32[128,8]{0,1:T(8,128)S(1)}, s32[128,8]{0,1:T(8,128)}, u32[]{:S(2)}) copy-start(s32[128,8]{0,1:T(8,128)} %param.9) | copy-start | bytes 12292
  126.1 18.8 %copy-start.6 = (f32[128,8]{0,1:T(8,128)S(1)}, f32[128,8]{0,1:T(8,128)}, u32[]{:S(2)}) copy-start(f32[128,8]{0,1:T(8,128)} %param.10) | copy-start | bytes 12292
  128.7 10.2 %all-to-all-start = ((f32[4,4,128]{2,0,1:T(4,128)}), f32[4,4,128]{2,0,1:T(4,128)S(1)}, u32[]{:S(2)}, u32[]{:S(2)}) async-start(f32[4,4,128]{2,0,1:T(4,128)} %bitcast.6), calls=%async_computation | async-start | bytes 16384 | tf_op jit(solution)/shard_map/all_to_all | solution.py:88
Sparse Core Ops, SparseCore 0:
  10.7 33.1 all-gather.1
  61.2 60.5 all-reduce.3

commit v2 on v1

v2 whole, which is shorter than its diff:
```python
import functools
import jax
import jax.numpy as jnp
from jax import lax
from jax.experimental import pallas as pl
from jax.experimental.pallas import tpu as pltpu
from jax.sharding import PartitionSpec as P

correction_multiplier = 2.0
bf16, f32 = jnp.bfloat16, jnp.float32


def dot(a, b, ca, cb):
    return lax.dot_general(a, b, (((ca,), (cb,)), ((), ())), preferred_element_type=f32)


def kernel(
    n_expert, n_dp,
    x_ref, routes_ref, gates_ref, h_ref, w_hbm, scale_ref, down_ref, up_ref,
    inter_ref, red_ref, exp_ref, out_ref,
    x_all, meta_send, meta_all, w_vmem, lines_ref, gcol_ref, dense_ref,
    hid, hid_sib, hid_chip, hid_x, row, row_sib, row_chip, row_x,
    fz, fz_sib, fz_chip, fz_x, dg_send, dg_recv, dg_part, dg_all,
    w_sem, ag_s, ag_r, mt_s, mt_r, hs_s, hs_r, hx_s, hx_r, rs_s, rs_r, rx_s, rx_r,
    fs_s, fs_r, fx_s, fx_r, ds_s, ds_r, dp_s, dp_r,
):
    exp_dev, hidden, width = w_vmem.shape
    slots = h_ref.shape[1]
    tok = x_ref.shape[0]
    capacity = slots // n_expert
    experts_all = exp_dev * n_expert
    top_count = routes_ref.shape[0]
    part = hidden // n_dp
    n_x = n_dp // 2
    me = lax.axis_index("expert")
    my_dp = lax.axis_index("dp")
    my_x, core = my_dp // 2, lax.rem(my_dp, 2)
    sibling = my_x * 2 + 1 - core
    blocked = capacity % 16 == 0

    for e in range(exp_dev):
        pltpu.make_async_copy(w_hbm.at[e], w_vmem.at[e], w_sem.at[e]).start()

    barrier = pltpu.get_barrier_semaphore()
    for d in range(1, n_expert):
        pl.semaphore_signal(barrier, inc=1, device_id={"expert": lax.rem(me + d, n_expert)})
    for d in range(1, n_dp):
        pl.semaphore_signal(barrier, inc=1, device_id={"dp": lax.rem(my_dp + d, n_dp)})

    ids = lax.broadcasted_iota(jnp.int32, (experts_all, tok), 0)
    named = jnp.zeros((experts_all, tok), f32)
    gate = jnp.zeros((experts_all, tok), f32)
    for k in range(top_count):
        eq = ids == routes_ref[k : k + 1, :]
        named = jnp.where(eq, 1.0, named)
        gate = jnp.where(eq, gates_ref[k : k + 1, :].astype(bf16).astype(f32), gate)
    earlier = (
        lax.broadcasted_iota(jnp.int32, (tok, tok), 0)
        < lax.broadcasted_iota(jnp.int32, (tok, tok), 1)
    )
    ranks = dot(named.astype(bf16), jnp.where(earlier, 1.0, 0.0).astype(bf16), 1, 0)
    ranks = jnp.where(named > 0.5, ranks, -1.0)
    for d in range(n_expert):
        meta_send[d, 0:exp_dev, :] = ranks[d * exp_dev : (d + 1) * exp_dev]
        meta_send[d, exp_dev : 2 * exp_dev, :] = gate[d * exp_dev : (d + 1) * exp_dev]

    pl.semaphore_wait(barrier, n_expert - 1 + n_dp - 1)

    def remote(src, dst, ss, rs, axis, peer):
        return pltpu.make_async_remote_copy(
            src_ref=src, dst_ref=dst, send_sem=ss, recv_sem=rs,
            device_id={axis: peer}, device_id_type=pl.DeviceIdType.MESH,
        )

    gathers = []
    for d in range(1, n_expert):
        to = lax.rem(me + d, n_expert)
        gathers.append(remote(meta_send.at[to], meta_all.at[me], mt_s.at[d], mt_r.at[d], "expert", to))
        gathers.append(remote(x_ref, x_all.at[me], ag_s.at[d], ag_r.at[d], "expert", to))
    for copy in gathers:
        copy.start()
    x_all[me] = x_ref[...]
    meta_all[me] = meta_send[me]

    for e in range(exp_dev):
        hid[e] = dot(down_ref[e], h_ref[e], 0, 1).astype(bf16)

    def pair(src, dst, ss, rs):
        return remote(src, dst, ss.at[0], rs.at[0], "dp", sibling)

    def across(src, dst, ss, rs):
        return [
            remote(src, dst.at[d], ss.at[d], rs.at[d], "dp", lax.rem(my_x + d, n_x) * 2 + core)
            for d in range(1, n_x)
        ]

    hid_pair = pair(hid, hid_sib, hs_s, hs_r)
    hid_pair.start()
    hid_pair.wait()
    hid_chip[...] = (hid[...].astype(f32) + hid_sib[...].astype(f32)).astype(bf16)
    hid_across = across(hid_chip, hid_x, hx_s, hx_r)
    for copy in hid_across:
        copy.start()
    for copy in gathers:
        copy.wait()

    def chosen(e, n):
        rows = capacity if blocked else slots
        place = lax.broadcasted_iota(jnp.int32, (rows, tok), 0).astype(f32)
        rank = meta_all[n, pl.ds(e, 1), :]
        if not blocked:
            rank = jnp.where(rank < 0.0, -1.0, rank + jnp.asarray(n * capacity, jnp.int32).astype(f32))
        return place == rank

    def gather_rows(e):
        if blocked:
            for n in range(n_expert):
                hit = chosen(e, n)
                lo = n * capacity
                lines_ref[e, lo : lo + capacity, :] = dot(
                    jnp.where(hit, 1.0, 0.0).astype(bf16), x_all[n], 1, 0
                ).astype(bf16)
                g = jnp.where(hit, meta_all[n, pl.ds(exp_dev + e, 1), :], 0.0)
                gcol_ref[e, lo : lo + capacity, :] = jnp.broadcast_to(
                    jnp.sum(g, axis=1, keepdims=True), (capacity, 128)
                )
        else:
            dense_ref[...] = jnp.zeros_like(dense_ref)
            gcol_ref[e] = jnp.zeros((slots, 128), f32)

            def step(n, carry):
                hit = chosen(e, n)
                dense_ref[...] += dot(jnp.where(hit, 1.0, 0.0).astype(bf16), x_all[n], 1, 0)
                g = jnp.where(hit, meta_all[n, pl.ds(exp_dev + e, 1), :], 0.0)
                gcol_ref[e] += jnp.broadcast_to(jnp.sum(g, axis=1, keepdims=True), (slots, 128))
                return carry

            lax.fori_loop(0, n_expert, step, 0)
            lines_ref[e] = dense_ref[...].astype(bf16)

    def fz_pair(e):
        return remote(fz.at[e, 1 - core], fz_sib.at[e], fs_s.at[e], fs_r.at[e], "dp", sibling)

    def fz_across(e):
        return [
            remote(
                fz_chip.at[e, d], fz_x.at[e, d], fx_s.at[e, d], fx_r.at[e, d],
                "dp", lax.rem(my_x + d, n_x) * 2 + core,
            )
            for d in range(1, n_x)
        ]

    def chip_sum(e, x):
        return fz[e, core, x].astype(f32) + fz_sib[e, x].astype(f32)

    def second(e):
        fz_pair(e).wait()
        for d in range(1, n_x):
            fz_chip[e, d] = chip_sum(e, lax.rem(my_x + d, n_x)).astype(bf16)
        for copy in fz_across(e):
            copy.start()

    def first(e, carry):
        gather_rows(e)
        lines = lines_ref[e]
        row[e] = dot(up_ref[e], lines, 1, 1).astype(bf16)
        scaled = (lines.astype(f32) * scale_ref[pl.ds(e, 1), :]).astype(bf16)
        pltpu.make_async_copy(w_hbm.at[e], w_vmem.at[e], w_sem.at[e]).wait()
        for q in range(n_dp):
            fz[e, q % 2, q // 2] = dot(
                w_vmem[e, q * part : (q + 1) * part, :], scaled, 1, 1
            ).astype(bf16)
        fz_pair(e).start()

        @pl.when(e > 0)
        def _():
            second(e - 1)

        return carry

    lax.fori_loop(0, exp_dev, first, 0)
    row_pair = pair(row, row_sib, rs_s, rs_r)
    row_pair.start()
    second(exp_dev - 1)
    row_pair.wait()
    row_chip[...] = (row[...].astype(f32) + row_sib[...].astype(f32)).astype(bf16)
    row_across = across(row_chip, row_x, rx_s, rx_r)
    for copy in row_across:
        copy.start()

    for copy in hid_across:
        copy.wait()

    def expander(e, carry):
        total = hid[e].astype(f32) + hid_sib[e].astype(f32)
        for d in range(1, n_x):
            total += hid_x[d, e].astype(f32)
        gate_row = jnp.transpose(gcol_ref[e])[0:1, :]
        exp_ref[e] = correction_multiplier * dot(
            (gate_row * total).astype(bf16), lines_ref[e], 1, 0
        )
        return carry

    lax.fori_loop(0, exp_dev, expander, 0)
    for copy in row_across:
        copy.wait()

    def last(e, carry):
        total = row[e].astype(f32) + row_sib[e].astype(f32)
        for d in range(1, n_x):
            total += row_x[d, e].astype(f32)
        row_proj = total.astype(bf16)
        gate_row = jnp.transpose(gcol_ref[e])[0:1, :]
        gated = (gate_row * row_proj.astype(f32)).astype(bf16)
        h = h_ref[e]
        red_ref[e] = correction_multiplier * dot(gated, h, 1, 0)
        for copy in fz_across(e):
            copy.wait()
        unit = chip_sum(e, my_x)
        for d in range(1, n_x):
            unit += fz_x[e, d].astype(f32)
        unit += correction_multiplier * dot(down_ref[e], row_proj, 1, 0)
        unit = jnp.transpose(unit)
        inter_ref[e] = (gcol_ref[e, :, 0:1] * unit).astype(bf16)
        dgate = jnp.sum(h.astype(f32) * unit, axis=1, keepdims=True)

        if blocked:
            for n in range(n_expert):
                lo = n * capacity
                dg_send[n, pl.ds(e, 1), :] = jnp.sum(
                    jnp.where(chosen(e, n), dgate[lo : lo + capacity], 0.0), axis=0, keepdims=True
                )
        else:
            def step(n, carry):
                dg_send[n, pl.ds(e, 1), :] = jnp.sum(
                    jnp.where(chosen(e, n), dgate, 0.0), axis=0, keepdims=True
                )
                return carry

            lax.fori_loop(0, n_expert, step, 0)
        return carry

    dg_send[...] = jnp.zeros_like(dg_send)
    lax.fori_loop(0, exp_dev, last, 0)

    back = []
    for d in range(1, n_expert):
        to = lax.rem(me + d, n_expert)
        back.append(remote(dg_send.at[to], dg_recv.at[me], ds_s.at[d], ds_r.at[d], "expert", to))
    for copy in back:
        copy.start()
    dg_recv[me] = dg_send[me]
    for copy in back:
        copy.wait()
    shares = [
        remote(dg_recv, dg_all.at[d], dp_s.at[d], dp_r.at[d], "dp", lax.rem(my_dp + d, n_dp))
        for d in range(1, n_dp)
    ]
    for copy in shares:
        copy.start()
    for copy in shares:
        copy.wait()
    order = [lax.rem(my_dp - p + n_dp, n_dp) for p in range(n_dp)]
    dg_all[0] = dg_recv[...]
    summed = dg_all[order[0]]
    for p in range(1, n_dp):
        summed += dg_all[order[p]]
    dg_part[...] = summed
    pair_dgate = jnp.zeros((top_count, tok), f32)
    for n in range(n_expert):
        for j in range(exp_dev):
            pair_dgate = jnp.where(
                routes_ref[...] == n * exp_dev + j, dg_part[n, j : j + 1, :], pair_dgate
            )
    weights = gates_ref[...]
    mean_term = jnp.sum(weights * pair_dgate, axis=0, keepdims=True)
    out_ref[...] = weights * (pair_dgate - mean_term)


def local(n_expert, n_dp, x, routes, gates, h, weight, scale, down, up):
    exp_dev, hidden, width = weight.shape
    slots = h.shape[1]
    tok, top_count = routes.shape
    rank = up.shape[1]
    part = hidden // n_dp
    n_x = n_dp // 2
    rows8 = -(-2 * exp_dev // 8) * 8
    blocked = (slots // n_expert) % 16 == 0
    vm = pltpu.VMEM
    dma = pltpu.SemaphoreType.DMA
    proj = (exp_dev, rank, slots)
    scratch = [
        vm((n_expert, tok, width), bf16), vm((n_expert, rows8, tok), f32),
        vm((n_expert, rows8, tok), f32), vm(weight.shape, bf16),
        vm((exp_dev, slots, width), bf16), vm((exp_dev, slots, 128), f32),
        vm((8, 128) if blocked else (slots, width), f32),
        vm(proj, bf16), vm(proj, bf16), vm(proj, bf16), vm((n_x,) + proj, bf16),
        vm(proj, bf16), vm(proj, bf16), vm(proj, bf16), vm((n_x,) + proj, bf16),
        vm((exp_dev, 2, n_x, part, slots), bf16), vm((exp_dev, n_x, part, slots), bf16),
        vm((exp_dev, n_x, part, slots), bf16), vm((exp_dev, n_x, part, slots), bf16),
        vm((n_expert, rows8, tok), f32), vm((n_expert, rows8, tok), f32),
        vm((n_expert, rows8, tok), f32), vm((n_dp, n_expert, rows8, tok), f32),
        dma((exp_dev,)),
        dma((n_expert,)), dma((n_expert,)), dma((n_expert,)), dma((n_expert,)),
        dma((1,)), dma((1,)), dma((n_x,)), dma((n_x,)),
        dma((1,)), dma((1,)), dma((n_x,)), dma((n_x,)),
        dma((exp_dev,)), dma((exp_dev,)), dma((exp_dev, n_x)), dma((exp_dev, n_x)),
        dma((n_expert,)), dma((n_expert,)), dma((n_dp,)), dma((n_dp,)),
    ]
    inside = pl.BlockSpec(memory_space=pltpu.VMEM)
    specs = [inside] * 8
    specs[4] = pl.BlockSpec(memory_space=pl.ANY)
    inter, red, expd, out = pl.pallas_call(
        functools.partial(kernel, n_expert, n_dp),
        out_shape=(
            jax.ShapeDtypeStruct(h.shape, bf16),
            jax.ShapeDtypeStruct((exp_dev, rank, part), f32),
            jax.ShapeDtypeStruct(up.shape, f32),
            jax.ShapeDtypeStruct((top_count, tok), f32),
        ),
        in_specs=specs,
        out_specs=(inside,) * 4,
        scratch_shapes=scratch,
        compiler_params=pltpu.CompilerParams(
            collective_id=0, has_side_effects=True, vmem_limit_bytes=52 * 2**20
        ),
    )(x, routes.T, gates.T, h, weight, scale, down, up)
    return inter, jnp.transpose(red, (0, 2, 1)), expd, out.T


def solution(mesh):
    return jax.shard_map(
        functools.partial(local, mesh.shape["expert"], mesh.shape["dp"]),
        mesh=mesh,
        in_specs=(
            P(("group", "expert"), "dp"),
            P(("group", "expert"), None),
            P(("group", "expert"), None),
            P(("group", "expert"), None, "dp"),
            P("expert", None, "dp"),
            P("expert", "dp"),
            P("expert", "dp", None),
            P("expert", None, "dp"),
        ),
        out_specs=(
            P(("group", "expert"), None, "dp"),
            P(("group", "expert"), "dp", None),
            P(("group", "expert"), None, "dp"),
            P(("group", "expert"), None),
        ),
        check_vma=False,
    )
```

time: 153 us -> 77.7 us (0.51)
  waiting for transfers between devices: 95.7 us -> 0 us
  Pallas kernels: 0 us -> 63.4 us
  matrix products: 17 us -> 0 us
  between operations: 14.9 us -> 0.65 us
  other arithmetic: 7.03 us -> 0 us
  blocking collectives: 6.05 us -> 0 us
  local copies, waits for them, and re-layouts: 7.15 us -> 13.2 us
  starting transfers between devices: 4.68 us -> 0 us
    pallas_call x0 -> x1, Pallas kernels: none -> 63.4 us  [local(): pl.pallas_call(functools.partial(kernel, n_expert, n_dp), out_shape=(jax....]
    unnamed x3 -> x0, waiting for transfers between devices: 59.4 us -> none
    all_gather x1 -> x0, waiting for transfers between devices: 31.8 us -> none  [local(): everyone = lax.all_gather(packed, 'expert', axis=0, tiled=True)]
    dot_general x8 -> x0, matrix products: 17 us -> none  [the longest x1 7.23 us: local(): jnp.einsum('esd,efd->fes', scaled, weight, preferred_element_type=f32)]
    unnamed x23 -> x16, local copies, waits for them, and re-layouts: 3.72 us -> 13.2 us
    psum x1 -> x0, blocking collectives: 6.05 us -> none  [local(): summed = lax.psum(returned, 'dp')]
    all_to_all x1 -> x0, starting transfers between devices: 4.6 us -> none  [local(): lax.all_to_all(token_dgate.reshape(exp_dev, n_expert, tok_rows), 'expert'...]
    all_to_all x1 -> x0, waiting for transfers between devices: 4.51 us -> none  [local(): lax.all_to_all(token_dgate.reshape(exp_dev, n_expert, tok_rows), 'expert'...]
  transfers between devices with their start and end apart: 3 -> 0, of which waited for: 3 -> 0; matrix products, arithmetic and copies ran while one was open for 2% -> 0% of each run, Pallas kernels for 0% -> 0%
where the time goes in v2:
time: 77.7 us; the launch traced here: 77.2 us
  Pallas kernels  63.4 us (82%)
  local copies, waits for them, and re-layouts  13.2 us (17%)
    pallas_call x1, Pallas kernels, local(): pl.pallas_call(functools.partial(kernel, n_expert, n_dp), out_shape=(jax....  63.4 us
    unnamed x16, local copies, waits for them, and re-layouts  13.2 us

profile of v2, /device:TPU:0, one launch (start us, length us, event | category | flops | bytes accessed | tf_op | source)
XLA Modules:
  0.0 77.2 jit_solution(5525059595041021719)
XLA Ops:
  0.6 1.1 %copy.13.down_ref = bf16[4,192,64]{2,1,0:T(8,128)(2,1)S(1)} copy(bf16[4,192,64]{1,2,0:T(8,128)(2,1)} %param.14) | data formatting | bytes 196608 | tf_op args[6]
  1.7 2.2 %copy.12.h_ref = bf16[4,384,192]{2,1,0:T(8,128)(2,1)} copy(bf16[4,384,192]{1,2,0:T(8,128)(2,1)} %param.11) | data formatting | bytes 1179648 | tf_op args[3]
  3.9 0.0 copy-start
  3.9 1.0 %copy-done = bf16[4,64,1024]{2,1,0:T(8,128)(2,1)S(1)} copy-done((bf16[4,64,1024]{2,1,0:T(8,128)(2,1)S(1)}, bf16[4,64,1024]{2,1,0:T(8,128)(2,1)}, u32[]{:S(2)}) %copy-start) | copy-done | bytes 524312
  5.0 0.0 copy-start.1
  5.0 0.9 %copy-done.1 = bf16[128,1024]{1,0:T(8,128)(2,1)S(1)} copy-done((bf16[128,1024]{1,0:T(8,128)(2,1)S(1)}, bf16[128,1024]{1,0:T(8,128)(2,1)}, u32[]{:S(2)}) %copy-start.1) | copy-done | bytes 262168
  5.9 0.0 copy-start.2
  5.9 0.7 copy-done.2
  6.6 0.0 copy-start.3
  6.6 0.7 copy-done.3
  7.3 0.0 copy-start.4
  7.3 0.7 copy-done.4
  8.0 63.4 %shard_map.111 = (bf16[4,384,192]{2,1,0:T(8,128)(2,1)}, f32[4,64,192]{2,1,0:T(8,128)S(1)}, f32[4,64,1024]{2,1,0:T(8,128)}, f32[8,128]{1,0:T(8,128)S(1)}) custom-call(bf16[128,1024]{1,0:T(8,128)(2,1)S(1)} %copy-done.1, s32[8,128]{1,0:T(8,128)S(1)} %bitcast.5, f32[8,128]{1,0:T(8,128)S(1)} %bitcast.6, bf16[4,384,192]{2,1,0:T(8,128)(2,1)} %copy.12.h_ref, ...), custom_call_target="tpu_custom_call" | custom-call | tf_op jit(solution)/shard_map/pallas_call | solution.py:313
  71.4 2.2 %copy.14 = bf16[4,384,192]{1,2,0:T(8,128)(2,1)} copy(bf16[4,384,192]{2,1,0:T(8,128)(2,1)} %get-tuple-element.12) | data formatting | bytes 1179648
  73.6 0.7 copy.18
  74.3 2.3 %copy.19 = f32[4,64,1024]{2,1,0:T(8,128)} copy(f32[4,64,1024]{2,1,0:T(8,128)} %get-tuple-element.22) | data formatting | bytes 2097152
  76.6 0.6 copy.20
Async XLA Ops:
  3.9 1.0 %copy-start = (bf16[4,64,1024]{2,1,0:T(8,128)(2,1)S(1)}, bf16[4,64,1024]{2,1,0:T(8,128)(2,1)}, u32[]{:S(2)}) copy-start(bf16[4,64,1024]{2,1,0:T(8,128)(2,1)} %up_ref.1) | copy-start | bytes 1572868
  5.0 0.9 %copy-start.1 = (bf16[128,1024]{1,0:T(8,128)(2,1)S(1)}, bf16[128,1024]{1,0:T(8,128)(2,1)}, u32[]{:S(2)}) copy-start(bf16[128,1024]{1,0:T(8,128)(2,1)} %x_ref.1) | copy-start | bytes 786436
  5.9 0.7 copy-start.2
  6.6 0.7 copy-start.3
  7.3 0.7 copy-start.4

commit v3 on v2

--- a/solution.py
+++ b/solution.py
@@ -16,16 +16,17 @@
 
 def kernel(
     n_expert, n_dp,
-    x_ref, routes_ref, gates_ref, h_ref, w_hbm, scale_ref, down_ref, up_ref,
+    x_ref, routes_hbm, gates_hbm, h_hbm, w_hbm, scale_hbm, down_hbm, up_hbm,
     inter_ref, red_ref, exp_ref, out_ref,
+    routes_ref, gates_ref, h_ref, scale_ref, down_ref, up_ref, in_sem, own_sem,
     x_all, meta_send, meta_all, w_vmem, lines_ref, gcol_ref, dense_ref,
     hid, hid_sib, hid_chip, hid_x, row, row_sib, row_chip, row_x,
     fz, fz_sib, fz_chip, fz_x, dg_send, dg_recv, dg_part, dg_all,
-    w_sem, ag_s, ag_r, mt_s, mt_r, hs_s, hs_r, hx_s, hx_r, rs_s, rs_r, rx_s, rx_r,
+    w_sem, right_s, right_r, left_s, left_r, mt_s, mt_r, hs_s, hs_r, hx_s, hx_r, rs_s, rs_r, rx_s, rx_r,
     fs_s, fs_r, fx_s, fx_r, ds_s, ds_r, dp_s, dp_r,
 ):
     exp_dev, hidden, width = w_vmem.shape
-    slots = h_ref.shape[1]
+    slots = h_ref.shape[2]
     tok = x_ref.shape[0]
     capacity = slots // n_expert
     experts_all = exp_dev * n_expert
@@ -38,6 +39,19 @@
     sibling = my_x * 2 + 1 - core
     blocked = capacity % 16 == 0
 
+    loads = [
+        pltpu.make_async_copy(src, dst, in_sem.at[i])
+        for i, (src, dst) in enumerate(
+            (
+                (routes_hbm, routes_ref), (gates_hbm, gates_ref), (h_hbm, h_ref),
+                (down_hbm, down_ref), (up_hbm, up_ref), (scale_hbm, scale_ref),
+            )
+        )
+    ]
+    for copy in loads:
+        copy.start()
+    own = pltpu.make_async_copy(x_ref, x_all.at[me], own_sem.at[0])
+    own.start()
     for e in range(exp_dev):
         pltpu.make_async_copy(w_hbm.at[e], w_vmem.at[e], w_sem.at[e]).start()
 
@@ -47,6 +61,8 @@
     for d in range(1, n_dp):
         pl.semaphore_signal(barrier, inc=1, device_id={"dp": lax.rem(my_dp + d, n_dp)})
 
+    loads[0].wait()
+    loads[1].wait()
     ids = lax.broadcasted_iota(jnp.int32, (experts_all, tok), 0)
     named = jnp.zeros((experts_all, tok), f32)
     gate = jnp.zeros((experts_all, tok), f32)
@@ -72,18 +88,45 @@
             device_id={axis: peer}, device_id_type=pl.DeviceIdType.MESH,
         )
 
+    def hop(k, way):
+        shard = me - way * (k - 1)
+        ss, rs = (right_s, right_r) if way > 0 else (left_s, left_r)
+        src = x_ref if k == 1 else x_all.at[shard]
+        sends = (me + way >= 0) & (me + way < n_expert) & (shard >= 0) & (shard < n_expert)
+        return sends, lambda: remote(
+            src, x_all.at[shard], ss.at[k], rs.at[k], "expert", me + way
+        )
+
+    def arrival(k, way):
+        shard = me - way * k
+        rs = right_r if way > 0 else left_r
+        ss = right_s if way > 0 else left_s
+        comes = (shard >= 0) & (shard < n_expert)
+        return shard, comes, lambda: remote(
+            x_all.at[shard], x_all.at[shard], ss.at[k], rs.at[k], "expert", me - way
+        )
+
+    def send(k, way):
+        sends, make = hop(k, way)
+
+        @pl.when(sends)
+        def _():
+            make().start()
+
     gathers = []
     for d in range(1, n_expert):
         to = lax.rem(me + d, n_expert)
         gathers.append(remote(meta_send.at[to], meta_all.at[me], mt_s.at[d], mt_r.at[d], "expert", to))
-        gathers.append(remote(x_ref, x_all.at[me], ag_s.at[d], ag_r.at[d], "expert", to))
+    send(1, 1)
+    send(1, -1)
     for copy in gathers:
         copy.start()
-    x_all[me] = x_ref[...]
     meta_all[me] = meta_send[me]
+    for copy in loads[2:]:
+        copy.wait()
 
     for e in range(exp_dev):
-        hid[e] = dot(down_ref[e], h_ref[e], 0, 1).astype(bf16)
+        hid[e] = dot(down_ref[e], h_ref[e], 1, 0).astype(bf16)
 
     def pair(src, dst, ss, rs):
         return remote(src, dst, ss.at[0], rs.at[0], "dp", sibling)
@@ -103,6 +146,7 @@
         copy.start()
     for copy in gathers:
         copy.wait()
+    own.wait()
 
     def chosen(e, n):
         rows = capacity if blocked else slots
@@ -112,19 +156,43 @@
             rank = jnp.where(rank < 0.0, -1.0, rank + jnp.asarray(n * capacity, jnp.int32).astype(f32))
         return place == rank
 
+    def gather_block(n):
+        def one(e, carry):
+            hit = chosen(e, n)
+            rows = pl.ds(pl.multiple_of(n * capacity, 16), capacity)
+            lines_ref[e, rows, :] = dot(
+                jnp.where(hit, 1.0, 0.0).astype(bf16), x_all[n], 1, 0
+            ).astype(bf16)
+            g = jnp.where(hit, meta_all[n, pl.ds(exp_dev + e, 1), :], 0.0)
+            gcol_ref[e, rows, :] = jnp.broadcast_to(
+                jnp.sum(g, axis=1, keepdims=True), (capacity, 128)
+            )
+            return carry
+
+        lax.fori_loop(0, exp_dev, one, 0)
+
+    if blocked:
+        gather_block(me)
+    for k in range(1, n_expert):
+        came = []
+        for way in (1, -1):
+            shard, comes, make = arrival(k, way)
+
+            @pl.when(comes)
+            def _():
+                make().wait_recv()
+
+            if k + 1 < n_expert:
+                send(k + 1, way)
+            came.append((shard, comes))
+        if blocked:
+            for shard, comes in came:
+                @pl.when(comes)
+                def _():
+                    gather_block(shard)
+
     def gather_rows(e):
-        if blocked:
-            for n in range(n_expert):
-                hit = chosen(e, n)
-                lo = n * capacity
-                lines_ref[e, lo : lo + capacity, :] = dot(
-                    jnp.where(hit, 1.0, 0.0).astype(bf16), x_all[n], 1, 0
-                ).astype(bf16)
-                g = jnp.where(hit, meta_all[n, pl.ds(exp_dev + e, 1), :], 0.0)
-                gcol_ref[e, lo : lo + capacity, :] = jnp.broadcast_to(
-                    jnp.sum(g, axis=1, keepdims=True), (capacity, 128)
-                )
-        else:
+        if not blocked:
             dense_ref[...] = jnp.zeros_like(dense_ref)
             gcol_ref[e] = jnp.zeros((slots, 128), f32)
 
@@ -213,16 +281,16 @@
         gate_row = jnp.transpose(gcol_ref[e])[0:1, :]
         gated = (gate_row * row_proj.astype(f32)).astype(bf16)
         h = h_ref[e]
-        red_ref[e] = correction_multiplier * dot(gated, h, 1, 0)
+        red_ref[e] = correction_multiplier * dot(gated, h, 1, 1)
         for copy in fz_across(e):
             copy.wait()
         unit = chip_sum(e, my_x)
         for d in range(1, n_x):
             unit += fz_x[e, d].astype(f32)
-        unit += correction_multiplier * dot(down_ref[e], row_proj, 1, 0)
-        unit = jnp.transpose(unit)
-        inter_ref[e] = (gcol_ref[e, :, 0:1] * unit).astype(bf16)
-        dgate = jnp.sum(h.astype(f32) * unit, axis=1, keepdims=True)
+        unit += correction_multiplier * dot(down_ref[e], row_proj, 0, 0)
+        inter_ref[e] = (gate_row * unit).astype(bf16)
+        dgate = jnp.sum(h.astype(f32) * unit, axis=0, keepdims=True)
+        dgate = jnp.transpose(jnp.broadcast_to(dgate, (128, slots)))[:, 0:1]
 
         if blocked:
             for n in range(n_expert):
@@ -242,6 +310,14 @@
 
     dg_send[...] = jnp.zeros_like(dg_send)
     lax.fori_loop(0, exp_dev, last, 0)
+
+    for k in range(1, n_expert):
+        for way in (1, -1):
+            sends, make = hop(k, way)
+
+            @pl.when(sends)
+            def _():
+                make().wait_send()
 
     back = []
     for d in range(1, n_expert):
@@ -278,8 +354,9 @@
 
 
 def local(n_expert, n_dp, x, routes, gates, h, weight, scale, down, up):
+    h, down = jnp.swapaxes(h, 1, 2), jnp.swapaxes(down, 1, 2)
     exp_dev, hidden, width = weight.shape
-    slots = h.shape[1]
+    slots = h.shape[2]
     tok, top_count = routes.shape
     rank = up.shape[1]
     part = hidden // n_dp
@@ -290,6 +367,8 @@
     dma = pltpu.SemaphoreType.DMA
     proj = (exp_dev, rank, slots)
     scratch = [
+        vm(routes.shape[::-1], jnp.int32), vm(gates.shape[::-1], f32), vm(h.shape, bf16),
+        vm(scale.shape, f32), vm(down.shape, bf16), vm(up.shape, bf16), dma((6,)), dma((1,)),
         vm((n_expert, tok, width), bf16), vm((n_expert, rows8, tok), f32),
         vm((n_expert, rows8, tok), f32), vm(weight.shape, bf16),
         vm((exp_dev, slots, width), bf16), vm((exp_dev, slots, 128), f32),
@@ -302,14 +381,13 @@
         vm((n_expert, rows8, tok), f32), vm((n_dp, n_expert, rows8, tok), f32),
         dma((exp_dev,)),
         dma((n_expert,)), dma((n_expert,)), dma((n_expert,)), dma((n_expert,)),
-        dma((1,)), dma((1,)), dma((n_x,)), dma((n_x,)),
+        dma((n_expert,)), dma((n_expert,)), dma((1,)), dma((1,)), dma((n_x,)), dma((n_x,)),
         dma((1,)), dma((1,)), dma((n_x,)), dma((n_x,)),
         dma((exp_dev,)), dma((exp_dev,)), dma((exp_dev, n_x)), dma((exp_dev, n_x)),
         dma((n_expert,)), dma((n_expert,)), dma((n_dp,)), dma((n_dp,)),
     ]
     inside = pl.BlockSpec(memory_space=pltpu.VMEM)
-    specs = [inside] * 8
-    specs[4] = pl.BlockSpec(memory_space=pl.ANY)
+    specs = [pl.BlockSpec(memory_space=pltpu.HBM)] * 8
     inter, red, expd, out = pl.pallas_call(
         functools.partial(kernel, n_expert, n_dp),
         out_shape=(
@@ -325,7 +403,7 @@
             collective_id=0, has_side_effects=True, vmem_limit_bytes=52 * 2**20
         ),
     )(x, routes.T, gates.T, h, weight, scale, down, up)
-    return inter, jnp.transpose(red, (0, 2, 1)), expd, out.T
+    return jnp.swapaxes(inter, 1, 2), jnp.transpose(red, (0, 2, 1)), expd, out.T
 
 
 def solution(mesh):

time: 77.7 us -> 70.9 us (0.912)
  local copies, waits for them, and re-layouts: 13.2 us -> 9.39 us
  Pallas kernels: 63.4 us -> 60.5 us
    unnamed x16, local copies, waits for them, and re-layouts: 13.2 us -> 9.39 us
    pallas_call x1, Pallas kernels: 63.4 us -> 60.5 us  [local(): pl.pallas_call(functools.partial(kernel, n_expert, n_dp), out_shape=(jax....]
where the time goes in v3:
time: 70.9 us; the launch traced here: 70.5 us
  Pallas kernels  60.5 us (85%)
  local copies, waits for them, and re-layouts  9.39 us (13%)
    pallas_call x1, Pallas kernels, local(): pl.pallas_call(functools.partial(kernel, n_expert, n_dp), out_shape=(jax....  60.5 us
    unnamed x16, local copies, waits for them, and re-layouts  9.39 us

profile of v3, /device:TPU:0, one launch (start us, length us, event | category | flops | bytes accessed | tf_op | source)
XLA Modules:
  0.0 70.5 jit_solution(5936793965521971829)
XLA Ops:
  0.6 0.0 copy-start
  0.6 1.0 %copy-done = bf16[4,64,1024]{2,1,0:T(8,128)(2,1)S(1)} copy-done((bf16[4,64,1024]{2,1,0:T(8,128)(2,1)S(1)}, bf16[4,64,1024]{2,1,0:T(8,128)(2,1)}, u32[]{:S(2)}) %copy-start) | copy-done | bytes 524312
  1.7 0.0 copy-start.1
  1.7 0.9 %copy-done.1 = bf16[128,1024]{1,0:T(8,128)(2,1)S(1)} copy-done((bf16[128,1024]{1,0:T(8,128)(2,1)S(1)}, bf16[128,1024]{1,0:T(8,128)(2,1)}, u32[]{:S(2)}) %copy-start.1) | copy-done | bytes 262168
  2.6 0.0 copy-start.2
  2.6 0.9 %copy-done.2 = bf16[4,192,64]{1,2,0:T(8,128)(2,1)S(1)} copy-done((bf16[4,192,64]{1,2,0:T(8,128)(2,1)S(1)}, bf16[4,192,64]{1,2,0:T(8,128)(2,1)}, u32[]{:S(2)}) %copy-start.2) | copy-done | bytes 98328
  3.5 0.0 copy-start.3
  3.5 0.7 %copy-done.3 = f32[4,1024]{1,0:T(4,128)S(1)} copy-done((f32[4,1024]{1,0:T(4,128)S(1)}, f32[4,1024]{1,0:T(4,128)}, u32[]{:S(2)}) %copy-start.3) | copy-done | bytes 16408
  4.2 0.0 copy-start.4
  4.3 0.7 copy-done.4
  4.9 0.0 copy-start.5
  4.9 0.7 copy-done.5
  5.6 60.5 %shard_map.111 = (bf16[4,192,384]{2,1,0:T(8,128)(2,1)S(1)}, f32[4,64,192]{2,1,0:T(8,128)S(1)}, f32[4,64,1024]{2,1,0:T(8,128)}, f32[8,128]{1,0:T(8,128)S(1)}) custom-call(bf16[128,1024]{1,0:T(8,128)(2,1)S(1)} %copy-done.1, s32[8,128]{1,0:T(8,128)S(1)} %bitcast.10, f32[8,128]{1,0:T(8,128)S(1)} %bitcast.11, bf16[4,192,384]{2,1,0:T(8,128)(2,1)} %bitcast.13, ...), custom_call_target="tpu_custom_call" | custom-call | tf_op jit(solution)/shard_map/pallas_call | solution.py:391
  66.1 0.8 %copy.16 = bf16[4,384,192]{1,2,0:T(8,128)(2,1)} copy(bf16[4,384,192]{1,2,0:T(8,128)(2,1)S(1)} %bitcast.7) | data formatting | bytes 1179648
  66.9 0.7 copy.17
  67.6 2.3 %copy.18 = f32[4,64,1024]{2,1,0:T(8,128)} copy(f32[4,64,1024]{2,1,0:T(8,128)} %get-tuple-element.18) | data formatting | bytes 2097152
  69.9 0.6 copy.19
Async XLA Ops:
  0.6 1.0 %copy-start = (bf16[4,64,1024]{2,1,0:T(8,128)(2,1)S(1)}, bf16[4,64,1024]{2,1,0:T(8,128)(2,1)}, u32[]{:S(2)}) copy-start(bf16[4,64,1024]{2,1,0:T(8,128)(2,1)} %up_hbm.1) | copy-start | bytes 1572868
  1.7 0.9 %copy-start.1 = (bf16[128,1024]{1,0:T(8,128)(2,1)S(1)}, bf16[128,1024]{1,0:T(8,128)(2,1)}, u32[]{:S(2)}) copy-start(bf16[128,1024]{1,0:T(8,128)(2,1)} %x_ref.1) | copy-start | bytes 786436
  2.6 0.9 %copy-start.2 = (bf16[4,192,64]{1,2,0:T(8,128)(2,1)S(1)}, bf16[4,192,64]{1,2,0:T(8,128)(2,1)}, u32[]{:S(2)}) copy-start(bf16[4,192,64]{1,2,0:T(8,128)(2,1)} %param.14) | copy-start | bytes 294916
  3.5 0.7 %copy-start.3 = (f32[4,1024]{1,0:T(4,128)S(1)}, f32[4,1024]{1,0:T(4,128)}, u32[]{:S(2)}) copy-start(f32[4,1024]{1,0:T(4,128)} %scale_hbm.1) | copy-start | bytes 49156
  4.2 0.7 copy-start.4
  4.9 0.7 copy-start.5

commit v4 on v3

--- a/solution.py
+++ b/solution.py
@@ -400,7 +400,7 @@
         out_specs=(inside,) * 4,
         scratch_shapes=scratch,
         compiler_params=pltpu.CompilerParams(
-            collective_id=0, has_side_effects=True, vmem_limit_bytes=52 * 2**20
+            collective_id=0, has_side_effects=True, vmem_limit_bytes=63 * 2**20
         ),
     )(x, routes.T, gates.T, h, weight, scale, down, up)
     return jnp.swapaxes(inter, 1, 2), jnp.transpose(red, (0, 2, 1)), expd, out.T

time: 70.9 us -> 68.9 us (0.972)
  local copies, waits for them, and re-layouts: 9.39 us -> 7.18 us
    unnamed x16 -> x4, local copies, waits for them, and re-layouts: 9.39 us -> 7.18 us
where the time goes in v4:
time: 68.9 us; the launch traced here: 68.7 us
  Pallas kernels  60.9 us (88%)
  local copies, waits for them, and re-layouts  7.18 us (10%)
    pallas_call x1, Pallas kernels, local(): pl.pallas_call(functools.partial(kernel, n_expert, n_dp), out_shape=(jax....  60.9 us
    unnamed x4, local copies, waits for them, and re-layouts  7.18 us

profile of v4, /device:TPU:0, one launch (start us, length us, event | category | flops | bytes accessed | tf_op | source)
XLA Modules:
  0.0 68.7 jit_solution(17423506694619142087)
XLA Ops:
  0.6 60.9 %shard_map.111 = (bf16[4,192,384]{2,1,0:T(8,128)(2,1)}, f32[4,64,192]{2,1,0:T(8,128)}, f32[4,64,1024]{2,1,0:T(8,128)}, f32[8,128]{1,0:T(8,128)}) custom-call(bf16[128,1024]{1,0:T(8,128)(2,1)} %x_ref.1, s32[8,128]{1,0:T(8,128)} %bitcast.11, f32[8,128]{1,0:T(8,128)} %bitcast.12, bf16[4,192,384]{2,1,0:T(8,128)(2,1)} %bitcast.7, bf16[4,768,1024]{2,1,0:T(8,128)(2,1)} %w_hbm.1, ...), custom_call_target="tpu_custom_call" | custom-call | tf_op jit(solution)/shard_map/pallas_call | solution.py:391
  61.5 1.9 %copy.16 = bf16[4,384,192]{1,2,0:T(8,128)(2,1)} copy(bf16[4,384,192]{1,2,0:T(8,128)(2,1)} %bitcast.8) | data formatting | bytes 1179648
  63.4 1.7 %copy.17 = f32[4,192,64]{1,2,0:T(8,128)} copy(f32[4,192,64]{1,2,0:T(8,128)} %bitcast.9) | data formatting | bytes 393216
  65.1 2.3 %copy.18 = f32[4,64,1024]{2,1,0:T(8,128)} copy(f32[4,64,1024]{2,1,0:T(8,128)} %get-tuple-element.18) | data formatting | bytes 2097152
  67.4 1.3 %copy.19 = f32[128,8]{0,1:T(8,128)} copy(f32[128,8]{0,1:T(8,128)} %bitcast.13) | data formatting | bytes 8192

commit v5 on v4

--- a/solution.py
+++ b/solution.py
@@ -18,7 +18,7 @@
     n_expert, n_dp,
     x_ref, routes_hbm, gates_hbm, h_hbm, w_hbm, scale_hbm, down_hbm, up_hbm,
     inter_ref, red_ref, exp_ref, out_ref,
-    routes_ref, gates_ref, h_ref, scale_ref, down_ref, up_ref, in_sem, own_sem,
+    routes_ref, gates_ref, h_ref, scale_ref, down_ref, up_ref, in_sem, own_sem, unit_ref,
     x_all, meta_send, meta_all, w_vmem, lines_ref, gcol_ref, dense_ref,
     hid, hid_sib, hid_chip, hid_x, row, row_sib, row_chip, row_x,
     fz, fz_sib, fz_chip, fz_x, dg_send, dg_recv, dg_part, dg_all,
@@ -156,56 +156,6 @@
             rank = jnp.where(rank < 0.0, -1.0, rank + jnp.asarray(n * capacity, jnp.int32).astype(f32))
         return place == rank
 
-    def gather_block(n):
-        def one(e, carry):
-            hit = chosen(e, n)
-            rows = pl.ds(pl.multiple_of(n * capacity, 16), capacity)
-            lines_ref[e, rows, :] = dot(
-                jnp.where(hit, 1.0, 0.0).astype(bf16), x_all[n], 1, 0
-            ).astype(bf16)
-            g = jnp.where(hit, meta_all[n, pl.ds(exp_dev + e, 1), :], 0.0)
-            gcol_ref[e, rows, :] = jnp.broadcast_to(
-                jnp.sum(g, axis=1, keepdims=True), (capacity, 128)
-            )
-            return carry
-
-        lax.fori_loop(0, exp_dev, one, 0)
-
-    if blocked:
-        gather_block(me)
-    for k in range(1, n_expert):
-        came = []
-        for way in (1, -1):
-            shard, comes, make = arrival(k, way)
-
-            @pl.when(comes)
-            def _():
-                make().wait_recv()
-
-            if k + 1 < n_expert:
-                send(k + 1, way)
-            came.append((shard, comes))
-        if blocked:
-            for shard, comes in came:
-                @pl.when(comes)
-                def _():
-                    gather_block(shard)
-
-    def gather_rows(e):
-        if not blocked:
-            dense_ref[...] = jnp.zeros_like(dense_ref)
-            gcol_ref[e] = jnp.zeros((slots, 128), f32)
-
-            def step(n, carry):
-                hit = chosen(e, n)
-                dense_ref[...] += dot(jnp.where(hit, 1.0, 0.0).astype(bf16), x_all[n], 1, 0)
-                g = jnp.where(hit, meta_all[n, pl.ds(exp_dev + e, 1), :], 0.0)
-                gcol_ref[e] += jnp.broadcast_to(jnp.sum(g, axis=1, keepdims=True), (slots, 128))
-                return carry
-
-            lax.fori_loop(0, n_expert, step, 0)
-            lines_ref[e] = dense_ref[...].astype(bf16)
-
     def fz_pair(e):
         return remote(fz.at[e, 1 - core], fz_sib.at[e], fs_s.at[e], fs_r.at[e], "dp", sibling)
 
@@ -228,10 +178,68 @@
         for copy in fz_across(e):
             copy.start()
 
+    def gather_block(n):
+        rows = pl.ds(pl.multiple_of(n * capacity, 16), capacity)
+        for e in range(exp_dev):
+            hit = chosen(e, n)
+            lines = dot(jnp.where(hit, 1.0, 0.0).astype(bf16), x_all[n], 1, 0)
+            lines_ref[e, rows, :] = lines.astype(bf16)
+            g = jnp.where(hit, meta_all[n, pl.ds(exp_dev + e, 1), :], 0.0)
+            gcol_ref[e, rows, :] = jnp.broadcast_to(
+                jnp.sum(g, axis=1, keepdims=True), (capacity, 128)
+            )
+            scaled = (lines * scale_ref[e : e + 1, :]).astype(bf16)
+            for q in range(n_dp):
+                fz[n, q % 2, q // 2, :, e * capacity : (e + 1) * capacity] = dot(
+                    w_vmem[e, q * part : (q + 1) * part, :], scaled, 1, 1
+                ).astype(bf16)
+        fz_pair(n).start()
+
+    if blocked:
+        for e in range(exp_dev):
+            pltpu.make_async_copy(w_hbm.at[e], w_vmem.at[e], w_sem.at[e]).wait()
+        gather_block(me)
+        second(me)
+    for k in range(1, n_expert):
+        came = []
+        for way in (1, -1):
+            shard, comes, make = arrival(k, way)
+
+            @pl.when(comes)
+            def _():
+                make().wait_recv()
+
+            if k + 1 < n_expert:
+                send(k + 1, way)
+            came.append((shard, comes))
+        if blocked:
+            for act in (gather_block, second):
+                for shard, comes in came:
+                    @pl.when(comes)
+                    def _():
+                        act(shard)
+
+    def gather_rows(e):
+        if not blocked:
+            dense_ref[...] = jnp.zeros_like(dense_ref)
+            gcol_ref[e] = jnp.zeros((slots, 128), f32)
+
+            def step(n, carry):
+                hit = chosen(e, n)
+                dense_ref[...] += dot(jnp.where(hit, 1.0, 0.0).astype(bf16), x_all[n], 1, 0)
+                g = jnp.where(hit, meta_all[n, pl.ds(exp_dev + e, 1), :], 0.0)
+                gcol_ref[e] += jnp.broadcast_to(jnp.sum(g, axis=1, keepdims=True), (slots, 128))
+                return carry
+
+            lax.fori_loop(0, n_expert, step, 0)
+            lines_ref[e] = dense_ref[...].astype(bf16)
+
     def first(e, carry):
         gather_rows(e)
         lines = lines_ref[e]
         row[e] = dot(up_ref[e], lines, 1, 1).astype(bf16)
+        if blocked:
+            return carry
         scaled = (lines.astype(f32) * scale_ref[pl.ds(e, 1), :]).astype(bf16)
         pltpu.make_async_copy(w_hbm.at[e], w_vmem.at[e], w_sem.at[e]).wait()
         for q in range(n_dp):
@@ -249,7 +257,8 @@
     lax.fori_loop(0, exp_dev, first, 0)
     row_pair = pair(row, row_sib, rs_s, rs_r)
     row_pair.start()
-    second(exp_dev - 1)
+    if not blocked:
+        second(exp_dev - 1)
     row_pair.wait()
     row_chip[...] = (row[...].astype(f32) + row_sib[...].astype(f32)).astype(bf16)
     row_across = across(row_chip, row_x, rx_s, rx_r)
@@ -282,12 +291,7 @@
         gated = (gate_row * row_proj.astype(f32)).astype(bf16)
         h = h_ref[e]
         red_ref[e] = correction_multiplier * dot(gated, h, 1, 1)
-        for copy in fz_across(e):
-            copy.wait()
-        unit = chip_sum(e, my_x)
-        for d in range(1, n_x):
-            unit += fz_x[e, d].astype(f32)
-        unit += correction_multiplier * dot(down_ref[e], row_proj, 0, 0)
+        unit = unit_ref[e] + correction_multiplier * dot(down_ref[e], row_proj, 0, 0)
         inter_ref[e] = (gate_row * unit).astype(bf16)
         dgate = jnp.sum(h.astype(f32) * unit, axis=0, keepdims=True)
         dgate = jnp.transpose(jnp.broadcast_to(dgate, (128, slots)))[:, 0:1]
@@ -307,6 +311,20 @@
 
             lax.fori_loop(0, n_expert, step, 0)
         return carry
+
+    for c in range(n_expert if blocked else exp_dev):
+        for copy in fz_across(c):
+            copy.wait()
+        total = chip_sum(c, my_x)
+        for d in range(1, n_x):
+            total += fz_x[c, d].astype(f32)
+        if blocked:
+            for e in range(exp_dev):
+                unit_ref[e, :, c * capacity : (c + 1) * capacity] = total[
+                    :, e * capacity : (e + 1) * capacity
+                ]
+        else:
+            unit_ref[c] = total
 
     dg_send[...] = jnp.zeros_like(dg_send)
     lax.fori_loop(0, exp_dev, last, 0)
@@ -363,27 +381,29 @@
     n_x = n_dp // 2
     rows8 = -(-2 * exp_dev // 8) * 8
     blocked = (slots // n_expert) % 16 == 0
+    chunks = n_expert if blocked else exp_dev
+    lanes = exp_dev * (slots // n_expert) if blocked else slots
     vm = pltpu.VMEM
     dma = pltpu.SemaphoreType.DMA
     proj = (exp_dev, rank, slots)
     scratch = [
         vm(routes.shape[::-1], jnp.int32), vm(gates.shape[::-1], f32), vm(h.shape, bf16),
-        vm(scale.shape, f32), vm(down.shape, bf16), vm(up.shape, bf16), dma((6,)), dma((1,)),
+        vm(scale.shape, f32), vm(down.shape, bf16), vm(up.shape, bf16), dma((6,)), dma((1,)), vm((exp_dev, part, slots), f32),
         vm((n_expert, tok, width), bf16), vm((n_expert, rows8, tok), f32),
         vm((n_expert, rows8, tok), f32), vm(weight.shape, bf16),
         vm((exp_dev, slots, width), bf16), vm((exp_dev, slots, 128), f32),
         vm((8, 128) if blocked else (slots, width), f32),
         vm(proj, bf16), vm(proj, bf16), vm(proj, bf16), vm((n_x,) + proj, bf16),
         vm(proj, bf16), vm(proj, bf16), vm(proj, bf16), vm((n_x,) + proj, bf16),
-        vm((exp_dev, 2, n_x, part, slots), bf16), vm((exp_dev, n_x, part, slots), bf16),
-        vm((exp_dev, n_x, part, slots), bf16), vm((exp_dev, n_x, part, slots), bf16),
+        vm((chunks, 2, n_x, part, lanes), bf16), vm((chunks, n_x, part, lanes), bf16),
+        vm((chunks, n_x, part, lanes), bf16), vm((chunks, n_x, part, lanes), bf16),
         vm((n_expert, rows8, tok), f32), vm((n_expert, rows8, tok), f32),
         vm((n_expert, rows8, tok), f32), vm((n_dp, n_expert, rows8, tok), f32),
         dma((exp_dev,)),
         dma((n_expert,)), dma((n_expert,)), dma((n_expert,)), dma((n_expert,)),
         dma((n_expert,)), dma((n_expert,)), dma((1,)), dma((1,)), dma((n_x,)), dma((n_x,)),
         dma((1,)), dma((1,)), dma((n_x,)), dma((n_x,)),
-        dma((exp_dev,)), dma((exp_dev,)), dma((exp_dev, n_x)), dma((exp_dev, n_x)),
+        dma((chunks,)), dma((chunks,)), dma((chunks, n_x)), dma((chunks, n_x)),
         dma((n_expert,)), dma((n_expert,)), dma((n_dp,)), dma((n_dp,)),
     ]
     inside = pl.BlockSpec(memory_space=pltpu.VMEM)

time: 68.9 us -> 64.5 us (0.936)
  Pallas kernels: 60.9 us -> 56.4 us
    pallas_call x1, Pallas kernels: 60.9 us -> 56.4 us  [local(): pl.pallas_call(functools.partial(kernel, n_expert, n_dp), out_shape=(jax....]
where the time goes in v5:
time: 64.5 us; the launch traced here: 64.2 us
  Pallas kernels  56.4 us (87%)
  local copies, waits for them, and re-layouts  7.18 us (11%)
    pallas_call x1, Pallas kernels, local(): pl.pallas_call(functools.partial(kernel, n_expert, n_dp), out_shape=(jax....  56.4 us
    unnamed x4, local copies, waits for them, and re-layouts  7.18 us

profile of v5, /device:TPU:0, one launch (start us, length us, event | category | flops | bytes accessed | tf_op | source)
XLA Modules:
  0.0 64.2 jit_solution(16327184748935133575)
XLA Ops:
  0.6 56.4 %shard_map.111 = (bf16[4,192,384]{2,1,0:T(8,128)(2,1)}, f32[4,64,192]{2,1,0:T(8,128)}, f32[4,64,1024]{2,1,0:T(8,128)}, f32[8,128]{1,0:T(8,128)}) custom-call(bf16[128,1024]{1,0:T(8,128)(2,1)} %x_ref.1, s32[8,128]{1,0:T(8,128)} %bitcast.11, f32[8,128]{1,0:T(8,128)} %bitcast.12, bf16[4,192,384]{2,1,0:T(8,128)(2,1)} %bitcast.7, bf16[4,768,1024]{2,1,0:T(8,128)(2,1)} %w_hbm.1, ...), custom_call_target="tpu_custom_call" | custom-call | tf_op jit(solution)/shard_map/pallas_call | solution.py:411
  57.1 1.9 %copy.16 = bf16[4,384,192]{1,2,0:T(8,128)(2,1)} copy(bf16[4,384,192]{1,2,0:T(8,128)(2,1)} %bitcast.8) | data formatting | bytes 1179648
  59.0 1.7 %copy.17 = f32[4,192,64]{1,2,0:T(8,128)} copy(f32[4,192,64]{1,2,0:T(8,128)} %bitcast.9) | data formatting | bytes 393216
  60.7 2.3 %copy.18 = f32[4,64,1024]{2,1,0:T(8,128)} copy(f32[4,64,1024]{2,1,0:T(8,128)} %get-tuple-element.18) | data formatting | bytes 2097152
  63.0 1.3 %copy.19 = f32[128,8]{0,1:T(8,128)} copy(f32[128,8]{0,1:T(8,128)} %bitcast.13) | data formatting | bytes 8192
